TPU v7x, 128 devices: a whole 4x4x4 slice. The times are simulated.
128 devices in a mesh: node: 32 (over y, x, z_lo), local: 4 (over z_hi, core).
Axes of the slice: x: 4, y: 4, z: 4 (z_hi: 2, z_lo: 2; z = z_hi * 2 + z_lo), core: 2. Of those that a mesh axis runs over, the one named last changes fastest.
Arguments:
- tokens: bfloat16 [16384, 4096], P(('node', 'local')), may hold values from -6 to 6
- grad_out: bfloat16 [16384, 4096], P(('node', 'local')), may hold values from -6 to 6
- router_logits: float32 [16384, 128], P(('node', 'local')), may hold values from -20 to 280
- group_id: int32 [16384], P(('node', 'local')), may hold values from 0 to 15, as said below
- expert_ids: int32 [16384, 2], P(('node', 'local')), may hold values from 0 to 7, as said below
- w_gate: bfloat16 [32, 4096, 1536], P('node', None, 'local'), may hold values from -0.09375 to 0.09375
- w_up: bfloat16 [32, 4096, 1536], P('node', None, 'local'), may hold values from -0.09375 to 0.09375
- w_down: bfloat16 [32, 1536, 4096], P('node', 'local'), may hold values from -0.15625 to 0.15625
Outputs:
- mixed: bfloat16 [16384, 4096], P(('node', 'local'))
- d_tokens: bfloat16 [16384, 4096], P(('node', 'local'))
- d_logits: float32 [16384, 128], P(('node', 'local'))
- grad_gate: bfloat16 [32, 4096, 1536], P('node', None, 'local')
- grad_up: bfloat16 [32, 4096, 1536], P('node', None, 'local')
- grad_down: bfloat16 [32, 1536, 4096], P('node', 'local')
Inputs may be any that keep to these rules, and one draw needn't show every extreme that they name: `group_id`: A token is computed here when its group is below 4. Among the tokens of one device no expert of those groups is named by more than 6 tokens, and one such expert is named by exactly 6 tokens of every device. `expert_ids`: the two numbers of a token differ; both name experts of the token's group.
All inputs are finite; a program needn't handle non-finite values.
Results may differ from a plain program's by a relative error of at most 0.0065.
Values may be sent and summed in bfloat16 or wider, within the bound.
No kernel may reach another device: no remote copies, remote signals or barrier semaphores. Data moves between devices by JAX's collectives and lax.ppermute only.
A program may use at most 192 MiB of HBM per device.

v0:
```python
import jax
import jax.numpy as jnp
from jax import lax
from jax.sharding import PartitionSpec as P

GSIZE = 8
CAP = 6


def cut_along(value, dim, length):
    lengths = value.shape
    pieces = value.reshape(*lengths[:dim], length, lengths[dim] // length, *lengths[dim + 1 :])
    return jnp.moveaxis(pieces, dim, 0)


def piece_ends(length, count):
    unit = 8 if length >= 8 * count else 1
    return [length // unit * k // count * unit for k in range(1, count)]


def in_order(pieces, dim):
    pieces = jnp.moveaxis(pieces, 0, dim)
    lengths = pieces.shape
    return pieces.reshape(*lengths[:dim], lengths[dim] * lengths[dim + 1], *lengths[dim + 2 :])


def exchange_in_pieces(value, axis, pieces, split_dim, concat_dim):
    blocks = cut_along(value, split_dim, lax.axis_size(axis))
    cut = max(range(1, max(2, blocks.ndim - 1)), key=lambda d: blocks.shape[d])
    outs = []
    for piece in jnp.split(blocks, piece_ends(blocks.shape[cut], pieces), axis=cut):
        if piece.size:
            outs.append(lax.all_to_all(piece, axis, split_axis=0, concat_axis=0, tiled=True))
    return in_order(jnp.concatenate(outs, axis=cut), concat_dim)


def gate_weights(logits, group_ids, chosen, inside):
    probabilities = jax.nn.softmax(logits, axis=-1)
    columns = jnp.arange(logits.shape[1], dtype=jnp.int32)
    member = ((columns // GSIZE)[None, :] == group_ids[:, None]).astype(logits.dtype)
    group_mass = jnp.sum(probabilities * member, axis=1)
    picked = jnp.sum(
        jnp.where(chosen[:, :, None] == columns[None, None, :], logits[:, None, :], 0.0), axis=2
    )
    pair_share = jax.nn.softmax(picked, axis=-1)
    return jnp.where(inside[:, None], group_mass[:, None] * pair_share, 0.0)


def spread(buffer):
    arrived = lax.all_to_all(buffer, "node", split_axis=0, concat_axis=2, tiled=True)
    arrived = lax.all_gather(arrived, "local", axis=2, tiled=True)
    return arrived[0]


def collect(partial_sums):
    summed = lax.psum_scatter(partial_sums[None], "local", scatter_dimension=2, tiled=True)
    result = exchange_in_pieces(summed.astype(jnp.bfloat16), "node", 2, 2, 0)
    return result.reshape(-1, result.shape[-1])


def body(tokens, grad_out, router_logits, group_id, expert_ids, w_gate, w_up, w_down):
    owned_count = w_gate.shape[0]
    node_count = lax.axis_size("node")
    expert_total = owned_count * node_count
    window_groups = expert_total // GSIZE
    model_width = tokens.shape[1]
    inside = group_id < window_groups
    chosen = group_id[:, None] * GSIZE + expert_ids
    target = jnp.where(inside[:, None], chosen, expert_total)
    expert_range = jnp.arange(expert_total, dtype=jnp.int32)
    onehot = (target[:, :, None] == expert_range[None, None, :]).astype(jnp.int32)
    per_token = jnp.sum(onehot, axis=1)
    earlier = jnp.cumsum(per_token, axis=0) - per_token
    slot_rank = jnp.sum(onehot * earlier[:, None, :], axis=2)
    slot_index = jnp.where(inside[:, None], target * CAP + slot_rank, -1)
    slot_range = jnp.arange(expert_total * CAP, dtype=jnp.int32)
    first_pick = (slot_range[:, None] == slot_index[None, :, 0]).astype(jnp.bfloat16)
    second_pick = (slot_range[:, None] == slot_index[None, :, 1]).astype(jnp.bfloat16)
    mix_weights, pull_back = jax.vjp(
        lambda values: gate_weights(values, group_id, chosen, inside), router_logits
    )
    grad_f32 = grad_out.astype(jnp.float32)
    first_grad = (mix_weights[:, 0:1] * grad_f32).astype(jnp.bfloat16)
    second_grad = (mix_weights[:, 1:2] * grad_f32).astype(jnp.bfloat16)
    send_rows = (
        jnp.dot(first_pick, tokens, preferred_element_type=jnp.float32)
        + jnp.dot(second_pick, tokens, preferred_element_type=jnp.float32)
    ).astype(jnp.bfloat16)
    send_grads = (
        jnp.dot(first_pick, first_grad, preferred_element_type=jnp.float32)
        + jnp.dot(second_pick, second_grad, preferred_element_type=jnp.float32)
    ).astype(jnp.bfloat16)
    buffer_shape = (node_count, owned_count, CAP, model_width)
    rows_in = spread(send_rows.reshape(buffer_shape))
    gate_pre = jnp.einsum("erd,edf->erf", rows_in, w_gate, preferred_element_type=jnp.float32)
    up_pre = jnp.einsum("erd,edf->erf", rows_in, w_up, preferred_element_type=jnp.float32)
    sigmoid_gate = jax.nn.sigmoid(gate_pre)
    activated = gate_pre * sigmoid_gate
    hidden = (activated * up_pre).astype(jnp.bfloat16)
    partial_out = jnp.einsum("erf,efd->erd", hidden, w_down, preferred_element_type=jnp.float32)
    out_flat = collect(partial_out)
    grads_in = spread(send_grads.reshape(buffer_shape))
    grad_hidden = jnp.einsum("erd,efd->erf", grads_in, w_down, preferred_element_type=jnp.float32)
    grad_gate_pre = (
        grad_hidden * up_pre * sigmoid_gate * (1.0 + gate_pre * (1.0 - sigmoid_gate))
    ).astype(jnp.bfloat16)
    grad_up_pre = (grad_hidden * activated).astype(jnp.bfloat16)
    partial_in = jnp.einsum(
        "erf,edf->erd", grad_gate_pre, w_gate, preferred_element_type=jnp.float32
    ) + jnp.einsum("erf,edf->erd", grad_up_pre, w_up, preferred_element_type=jnp.float32)
    back_flat = collect(partial_in)
    grad_gate = jnp.einsum(
        "erd,erf->edf", rows_in, grad_gate_pre, preferred_element_type=jnp.float32
    ).astype(jnp.bfloat16)
    grad_up = jnp.einsum(
        "erd,erf->edf", rows_in, grad_up_pre, preferred_element_type=jnp.float32
    ).astype(jnp.bfloat16)
    grad_down = jnp.einsum(
        "erf,erd->efd", hidden, grads_in, preferred_element_type=jnp.float32
    ).astype(jnp.bfloat16)
    first_out = jnp.einsum("st,sd->td", first_pick, out_flat, preferred_element_type=jnp.float32)
    second_out = jnp.einsum("st,sd->td", second_pick, out_flat, preferred_element_type=jnp.float32)
    first_back = jnp.einsum("st,sd->td", first_pick, back_flat, preferred_element_type=jnp.float32)
    second_back = jnp.einsum(
        "st,sd->td", second_pick, back_flat, preferred_element_type=jnp.float32
    )
    mixed = (mix_weights[:, 0:1] * first_out + mix_weights[:, 1:2] * second_out).astype(
        jnp.bfloat16
    )
    d_tokens = (first_back + second_back).astype(jnp.bfloat16)
    scores = jnp.stack(
        [jnp.sum(grad_f32 * first_out, axis=1), jnp.sum(grad_f32 * second_out, axis=1)], axis=1
    )
    d_logits = pull_back(scores)[0]
    return (mixed, d_tokens, d_logits, grad_gate, grad_up, grad_down)


def solution(mesh):
    return jax.shard_map(
        body,
        mesh=mesh,
        in_specs=(
            P(("node", "local"), None),
            P(("node", "local"), None),
            P(("node", "local"), None),
            P(("node", "local")),
            P(("node", "local"), None),
            P("node", None, "local"),
            P("node", None, "local"),
            P("node", "local", None),
        ),
        out_specs=(
            P(("node", "local"), None),
            P(("node", "local"), None),
            P(("node", "local"), None),
            P("node", None, "local"),
            P("node", None, "local"),
            P("node", "local", None),
        ),
        check_vma=False,
    )
```

profile of v0, /device:TPU:0, one launch (start us, length us, event | category | flops | bytes accessed | tf_op | source)
XLA Modules:
  0.0 582.0 jit_solution(17738413348024515923)
XLA Ops:
  13.5 3.5 reshape.156
  17.0 37.9 %all_to_all.44 = bf16[32,1,6,4096]{3,2,1,0:T(8,128)(2,1)} all-to-all(bf16[32,1,6,4096]{3,2,1,0:T(8,128)(2,1)} %bitcast.95), channel_id=1, replica_groups=mesh['node'=32,'local'=4] {'node'}, dimensions={0} | all-to-all | bytes 3145728 | tf_op jit(solution)/shard_map/all_to_all | solution.py:50
  54.9 3.7 all_to_all.31
  58.7 48.7 %all-gather.3.cloned.1.call-done = bf16[1,1,768,4096]{3,2,1,0:T(8,128)(2,1)} async-done(((bf16[1,1,192,4096]{3,2,1,0:T(8,128)(2,1)}), bf16[1,1,768,4096]{3,2,1,0:T(8,128)(2,1)}) %all-gather.3.cloned.1.call-update) | async-done | bytes 6291472 | tf_op jit(solution)/shard_map/all_gather | solution.py:51
  107.4 6.6 %fusion.10 = f32[768,384]{1,0:T(8,128)S(1)} fusion(bf16[1,1,768,4096]{3,2,1,0:T(8,128)(2,1)} %all-gather.3.cloned.1.call-done, bf16[1,4096,384]{2,1,0:T(8,128)(2,1)} %param.13), kind=kOutput, calls=%fused_computation.12 | convolution fusion | flops 2415919104 | bytes 10616832 | tf_op jit(solution)/shard_map/erd,edf->erf/dot_general | solution.py:95
  114.0 4.5 multiply_convert_fusion.2
  119.3 6.4 %convolution_bitcast_fusion = f32[1,1,768,4096]{3,2,1,0:T(8,128)} fusion(bf16[768,384]{1,0:T(8,128)(2,1)S(1)} %get-tuple-element.26, bf16[1,384,4096]{2,1,0:T(8,128)(2,1)S(1)} %copy-done), kind=kOutput, calls=%fused_computation.1 | convolution fusion | flops 2415919104 | bytes 16318464 | tf_op jit(solution)/shard_map/erf,efd->erd/dot_general | solution.py:100
  125.8 105.4 %reduce-scatter.3.cloned.1.call-done = f32[1,1,192,4096]{3,2,1,0:T(8,128)} async-done(((f32[1,1,768,4096]{3,2,1,0:T(8,128)}), f32[1,1,192,4096]{3,2,1,0:T(8,128)}) %reduce-scatter.3.cloned.1.call-update) | async-done | bytes 3145744 | tf_op jit(solution)/shard_map/reduce_scatter | solution.py:56
  234.4 3.5 transpose_reshape.6
  237.9 4.7 slice_bitcast_fusion.3
  242.6 7.4 %all-to-all-start.1 = ((bf16[32,1,1,3,4096]{4,3,2,1,0:T(4,128)(2,1)}), bf16[32,1,1,3,4096]{4,3,2,1,0:T(4,128)(2,1)}, u32[]{:S(2)}, u32[]{:S(2)}) async-start(bf16[32,1,1,3,4096]{4,3,2,1,0:T(4,128)(2,1)} %get-tuple-element.18), calls=%async_computation.2 | async-start | bytes 2097152 | tf_op jit(solution)/shard_map/all_to_all | solution.py:33
  250.4 17.5 %all-to-all-done.1 = bf16[32,1,1,3,4096]{4,3,2,1,0:T(4,128)(2,1)} async-done(((bf16[32,1,1,3,4096]{4,3,2,1,0:T(4,128)(2,1)}), bf16[32,1,1,3,4096]{4,3,2,1,0:T(4,128)(2,1)}, u32[]{:S(2)}, u32[]{:S(2)}) %all-to-all-start.1) | async-done | bytes 786464 | tf_op jit(solution)/shard_map/all_to_all | solution.py:33
  267.9 4.7 all-to-all-start.2
  272.6 10.2 %all-gather.5.cloned.1.call-start = ((), (), s32[]{:S(2)}) async-start(), calls=%async_computation.10 | async-start | bytes 7864320 | tf_op jit(solution)/shard_map/all_gather | solution.py:51
  283.0 6.4 %all-to-all-done.2 = bf16[32,1,1,3,4096]{4,3,2,1,0:T(4,128)(2,1)} async-done(((bf16[32,1,1,3,4096]{4,3,2,1,0:T(4,128)(2,1)}), bf16[32,1,1,3,4096]{4,3,2,1,0:T(4,128)(2,1)}, u32[]{:S(2)}, u32[]{:S(2)}) %all-to-all-start.2) | async-done | bytes 786464 | tf_op jit(solution)/shard_map/all_to_all | solution.py:33
  289.4 3.9 pad_maximum_fusion
  293.3 3.7 reshape_reshape.6
  304.1 3.5 reshape.161
  307.6 31.9 %all_to_all.45 = bf16[32,1,6,4096]{3,2,1,0:T(8,128)(2,1)} all-to-all(bf16[32,1,6,4096]{3,2,1,0:T(8,128)(2,1)} %bitcast.96), channel_id=1, replica_groups=mesh['node'=32,'local'=4] {'node'}, dimensions={0} | all-to-all | bytes 3145728 | tf_op jit(solution)/shard_map/all_to_all | solution.py:50
  339.5 3.7 all_to_all.35
  343.2 47.0 %all-gather.5.cloned.1.call-done = bf16[1,1,768,4096]{3,2,1,0:T(8,128)(2,1)} async-done(((bf16[1,1,192,4096]{3,2,1,0:T(8,128)(2,1)}), bf16[1,1,768,4096]{3,2,1,0:T(8,128)(2,1)}) %all-gather.5.cloned.1.call-update) | async-done | bytes 6291472 | tf_op jit(solution)/shard_map/all_gather | solution.py:51
  390.3 7.3 %multiply_convert_fusion = (bf16[768,384]{1,0:T(8,128)(2,1)S(1)}, bf16[768,384]{1,0:T(8,128)(2,1)S(1)}) fusion(f32[768,384]{1,0:T(8,128)} %copy-done.20, f32[768,384]{1,0:T(8,128)} %get-tuple-element.27, bf16[1,384,4096]{2,1,0:T(8,128)(2,1)S(1)} %copy-done, bf16[1,1,768,4096]{3,2,1,0:T(8,128)(2,1)} %all-gather.5.cloned.1.call-done), kind=kOutput, calls=%fused_computation.44 | convolution fusion | flops 2419752960 | bytes 12976128 | tf_op jit(solution)/shard_map/erd,efd->erf/dot_general | solution.py:103
  397.6 3.5 fusion.37
  401.1 6.5 %add_bitcast_fusion = f32[1,1,768,4096]{3,2,1,0:T(8,128)} fusion(f32[768,4096]{1,0:T(8,128)S(1)} %fusion.37, bf16[768,384]{1,0:T(8,128)(2,1)S(1)} %get-tuple-element.14, bf16[1,4096,384]{2,1,0:T(8,128)(2,1)S(1)} %copy-done.11), kind=kOutput, calls=%fused_computation | convolution fusion | flops 2419064832 | bytes 28901376 | tf_op jit(solution)/shard_map/erf,edf->erd/dot_general | solution.py:110
  412.2 100.9 %reduce-scatter.5.cloned.1.call-done = f32[1,1,192,4096]{3,2,1,0:T(8,128)} async-done(((f32[1,1,768,4096]{3,2,1,0:T(8,128)}), f32[1,1,192,4096]{3,2,1,0:T(8,128)}) %reduce-scatter.5.cloned.1.call-update) | async-done | bytes 3145744 | tf_op jit(solution)/shard_map/reduce_scatter | solution.py:56
  513.1 3.2 convert_element_type.74
  521.2 7.5 %all-to-all-start.4 = ((bf16[32,1,1,3,4096]{4,3,2,1,0:T(4,128)(2,1)}), bf16[32,1,1,3,4096]{4,3,2,1,0:T(4,128)(2,1)S(1)}, u32[]{:S(2)}, u32[]{:S(2)}) async-start(bf16[32,1,1,3,4096]{4,3,2,1,0:T(4,128)(2,1)} %get-tuple-element.16), calls=%async_computation.6 | async-start | bytes 2097152 | tf_op jit(solution)/shard_map/all_to_all | solution.py:33
  529.5 7.9 %fusion.24 = bf16[1,4096,384]{2,1,0:T(8,128)(2,1)} fusion(bf16[768,384]{1,0:T(8,128)(2,1)S(1)} %copy-done.15, bf16[1,1,768,4096]{3,2,1,0:T(8,128)(2,1)} %all-gather.3.cloned.1.call-done), kind=kOutput, calls=%fused_computation.20 | convolution fusion | flops 2417491968 | bytes 10027008 | tf_op jit(solution)/shard_map/erd,erf->edf/dot_general | solution.py:115
  537.5 8.9 %all-to-all-done.4 = bf16[32,1,1,3,4096]{4,3,2,1,0:T(4,128)(2,1)S(1)} async-done(((bf16[32,1,1,3,4096]{4,3,2,1,0:T(4,128)(2,1)}), bf16[32,1,1,3,4096]{4,3,2,1,0:T(4,128)(2,1)S(1)}, u32[]{:S(2)}, u32[]{:S(2)}) %all-to-all-start.4) | async-done | bytes 786464 | tf_op jit(solution)/shard_map/all_to_all | solution.py:33
  546.4 4.7 all-to-all-start.5
  551.1 7.2 %fusion.21 = bf16[1,384,4096]{2,1,0:T(8,128)(2,1)} fusion(bf16[768,384]{1,0:T(8,128)(2,1)S(1)} %copy-done.9, bf16[1,1,768,4096]{3,2,1,0:T(8,128)(2,1)} %all-gather.5.cloned.1.call-done), kind=kOutput, calls=%fused_computation.19 | convolution fusion | flops 2417491968 | bytes 10027008 | tf_op jit(solution)/shard_map/erf,erd->efd/dot_general | solution.py:118
  558.3 7.9 %fusion.27 = bf16[1,4096,384]{2,1,0:T(8,128)(2,1)} fusion(bf16[768,384]{1,0:T(8,128)(2,1)S(1)} %copy-done.17, bf16[1,1,768,4096]{3,2,1,0:T(8,128)(2,1)} %all-gather.3.cloned.1.call-done), kind=kOutput, calls=%fused_computation.21 | convolution fusion | flops 2417491968 | bytes 10027008 | tf_op jit(solution)/shard_map/erd,erf->edf/dot_general | solution.py:112
  (92 shorter events, 37.3 us)
Async XLA Ops:
  7.2 112.2 %copy-start = (bf16[1,384,4096]{2,1,0:T(8,128)(2,1)S(1)}, bf16[1,384,4096]{2,1,0:T(8,128)(2,1)}, u32[]{:S(2)}) copy-start(bf16[1,384,4096]{2,1,0:T(8,128)(2,1)} %param.15) | copy-start | bytes 9437188
  7.2 100.2 %all-gather.3.cloned.1.call-start = ((), (), s32[]{:S(2)}) async-start(), calls=%async_computation.8 | async-start | bytes 7864320 | tf_op jit(solution)/shard_map/all_gather | solution.py:51
  9.9 1.9 copy-start.7
  58.6 172.6 %reduce-scatter.3.cloned.1.call-start = ((), (), s32[]{:S(2)}) async-start(), calls=%async_computation.9 | async-start | bytes 15728640 | tf_op jit(solution)/shard_map/reduce_scatter | solution.py:56
  107.4 6.6 %copy-start.10 = (bf16[1,4096,384]{2,1,0:T(8,128)(2,1)S(1)}, bf16[1,4096,384]{2,1,0:T(8,128)(2,1)}, u32[]{:S(2)}) copy-start(bf16[1,4096,384]{2,1,0:T(8,128)(2,1)} %param.14) | copy-start | bytes 9437188
  107.4 6.6 %copy-start.19 = (bf16[1,1,768,4096]{3,2,1,0:T(8,128)(2,1)S(1)}, bf16[1,1,768,4096]{3,2,1,0:T(8,128)(2,1)}, u32[]{:S(2)}) copy-start(bf16[1,1,768,4096]{3,2,1,0:T(8,128)(2,1)} %all-gather.3.cloned.1.call-done) | copy-start | bytes 18874372
  114.0 4.5 copy-start.20
  118.5 0.8 copy-start.8
  242.6 7.5 %copy-start.13 = (f32[128,128]{1,0:T(8,128)S(1)}, f32[128,128]{1,0:T(8,128)}, u32[]{:S(2)}) copy-start(f32[128,128]{1,0:T(8,128)} %param.10) | copy-start | bytes 196612
  242.6 25.3 %all-to-all-start.1 = ((bf16[32,1,1,3,4096]{4,3,2,1,0:T(4,128)(2,1)}), bf16[32,1,1,3,4096]{4,3,2,1,0:T(4,128)(2,1)}, u32[]{:S(2)}, u32[]{:S(2)}) async-start(bf16[32,1,1,3,4096]{4,3,2,1,0:T(4,128)(2,1)} %get-tuple-element.18), calls=%async_computation.2 | async-start | bytes 2097152 | tf_op jit(solution)/shard_map/all_to_all | solution.py:33
  267.9 21.5 %all-to-all-start.2 = ((bf16[32,1,1,3,4096]{4,3,2,1,0:T(4,128)(2,1)}), bf16[32,1,1,3,4096]{4,3,2,1,0:T(4,128)(2,1)}, u32[]{:S(2)}, u32[]{:S(2)}) async-start(bf16[32,1,1,3,4096]{4,3,2,1,0:T(4,128)(2,1)} %get-tuple-element.19), calls=%async_computation.3 | async-start | bytes 2097152 | tf_op jit(solution)/shard_map/all_to_all | solution.py:33
  272.6 117.7 %all-gather.5.cloned.1.call-start = ((), (), s32[]{:S(2)}) async-start(), calls=%async_computation.10 | async-start | bytes 7864320 | tf_op jit(solution)/shard_map/all_gather | solution.py:51
  297.0 2.1 copy-start.5
  297.0 2.2 copy-start.6
  299.1 2.2 copy-start.2
  299.1 2.2 copy-start.18
  343.2 169.9 %reduce-scatter.5.cloned.1.call-start = ((), (), s32[]{:S(2)}) async-start(), calls=%async_computation.11 | async-start | bytes 15728640 | tf_op jit(solution)/shard_map/reduce_scatter | solution.py:56
  390.3 7.3 %copy-start.12 = (bf16[1,4096,384]{2,1,0:T(8,128)(2,1)S(1)}, bf16[1,4096,384]{2,1,0:T(8,128)(2,1)}, u32[]{:S(2)}) copy-start(bf16[1,4096,384]{2,1,0:T(8,128)(2,1)} %param.13) | copy-start | bytes 9437188
  397.6 3.5 copy-start.16
  397.6 3.5 copy-start.14
  397.6 3.5 copy-start.11
  407.6 1.6 copy-start.3
  521.2 8.3 %copy-start.15 = (bf16[768,384]{1,0:T(8,128)(2,1)S(1)}, bf16[768,384]{1,0:T(8,128)(2,1)}, u32[]{:S(2)}) copy-start(bf16[768,384]{1,0:T(8,128)(2,1)} %copy-done.14) | copy-start | bytes 1769476
  521.2 25.2 %all-to-all-start.4 = ((bf16[32,1,1,3,4096]{4,3,2,1,0:T(4,128)(2,1)}), bf16[32,1,1,3,4096]{4,3,2,1,0:T(4,128)(2,1)S(1)}, u32[]{:S(2)}, u32[]{:S(2)}) async-start(bf16[32,1,1,3,4096]{4,3,2,1,0:T(4,128)(2,1)} %get-tuple-element.16), calls=%async_computation.6 | async-start | bytes 2097152 | tf_op jit(solution)/shard_map/all_to_all | solution.py:33
  537.5 13.6 %copy-start.9 = (bf16[768,384]{1,0:T(8,128)(2,1)S(1)}, bf16[768,384]{1,0:T(8,128)(2,1)}, u32[]{:S(2)}) copy-start(bf16[768,384]{1,0:T(8,128)(2,1)} %copy-done.8) | copy-start | bytes 1769476
  546.4 21.5 %all-to-all-start.5 = ((bf16[32,1,1,3,4096]{4,3,2,1,0:T(4,128)(2,1)}), bf16[32,1,1,3,4096]{4,3,2,1,0:T(4,128)(2,1)}, u32[]{:S(2)}, u32[]{:S(2)}) async-start(bf16[32,1,1,3,4096]{4,3,2,1,0:T(4,128)(2,1)} %get-tuple-element.17), calls=%async_computation.7 | async-start | bytes 2097152 | tf_op jit(solution)/shard_map/all_to_all | solution.py:33
  551.1 7.2 %copy-start.17 = (bf16[768,384]{1,0:T(8,128)(2,1)S(1)}, bf16[768,384]{1,0:T(8,128)(2,1)}, u32[]{:S(2)}) copy-start(bf16[768,384]{1,0:T(8,128)(2,1)} %copy-done.16) | copy-start | bytes 1769476
  571.6 2.1 copy-start.4
  571.6 3.5 copy-start.1
Sparse Core Ops, SparseCore 0:
  58.7 48.6 all-gather.2
  125.9 105.2 reduce-scatter.2
  343.3 46.9 all-gather.4
  407.7 105.3 reduce-scatter.4
where the time goes:
time: 591 us; the launch traced here: 582 us
  waiting for transfers between devices  337 us (57%)
  matrix products  71.5 us (12%)
  blocking collectives  69.8 us (12%)
  local copies, waits for them, and re-layouts  35.1 us (6%)
  starting transfers between devices  34.6 us (6%)
  other arithmetic  19.9 us (3%)
  between operations  14.5 us (2%)
    reduce_scatter x2, waiting for transfers between devices, collect(): lax.psum_scatter(partial_sums[None], 'local', scatter_dimension=2, tiled=...  206 us
    all_gather x2, waiting for transfers between devices, spread(): arrived = lax.all_gather(arrived, 'local', axis=2, tiled=True)  95.8 us
    all_to_all x2, blocking collectives, spread(): lax.all_to_all(buffer, 'node', split_axis=0, concat_axis=2, tiled=True)  69.8 us
    all_to_all x4, waiting for transfers between devices, exchange_in_pieces(): lax.all_to_all(piece, axis, split_axis=0, concat_axis=0, tiled=True)  34.5 us
    all_to_all x4, starting transfers between devices, exchange_in_pieces(): lax.all_to_all(piece, axis, split_axis=0, concat_axis=0, tiled=True)  24.3 us
  transfers between devices with their start and end apart: 8, of which 8 were waited for; matrix products, arithmetic and copies ran while one was open for 5% of the time, Pallas kernels for 0%

commit v1 on v0

--- a/solution.py
+++ b/solution.py
@@ -48,7 +48,9 @@
 
 def spread(buffer):
     arrived = lax.all_to_all(buffer, "node", split_axis=0, concat_axis=2, tiled=True)
-    arrived = lax.all_gather(arrived, "local", axis=2, tiled=True)
+    arrived = jnp.concatenate(
+        lax.all_to_all(jnp.stack([arrived] * lax.axis_size("local")), "local", 0, 0), axis=2
+    )
     return arrived[0]
 
 

time: 591 us -> 650 us (1.100)
  blocking collectives: 69.8 us -> 222 us
  waiting for transfers between devices: 337 us -> 243 us
  matrix products: 71.5 us -> 64.7 us
    all_to_all x0 -> x2, blocking collectives: none -> 152 us  [spread(): lax.all_to_all(jnp.stack([arrived] * lax.axis_size('local')), 'local', 0, 0)]
    all_gather x2 -> x0, waiting for transfers between devices: 95.8 us -> none  [spread(): arrived = lax.all_gather(arrived, 'local', axis=2, tiled=True)]
    another operation x0 -> x4, local copies, waits for them, and re-layouts: none -> 11.7 us  [spread(): jnp.stack([arrived] * lax.axis_size('local'))]
    all_to_all x4, starting transfers between devices: 24.3 us -> 34.8 us  [exchange_in_pieces(): lax.all_to_all(piece, axis, split_axis=0, concat_axis=0, tiled=True)]
    all_gather x2 -> x0, starting transfers between devices: 10.2 us -> none  [spread(): arrived = lax.all_gather(arrived, 'local', axis=2, tiled=True)]
    all_to_all x4, waiting for transfers between devices: 34.5 us -> 44.6 us  [exchange_in_pieces(): lax.all_to_all(piece, axis, split_axis=0, concat_axis=0, tiled=True)]
    reduce_scatter x2, waiting for transfers between devices: 206 us -> 198 us  [collect(): lax.psum_scatter(partial_sums[None], 'local', scatter_dimension=2, tiled=...]
    all_to_all x2 -> x0, local copies, waits for them, and re-layouts: 7.32 us -> none  [spread(): lax.all_to_all(buffer, 'node', split_axis=0, concat_axis=2, tiled=True)]
  transfers between devices with their start and end apart: 8 -> 6, of which waited for: 8 -> 6; matrix products, arithmetic and copies ran while one was open for 5% -> 4% of each run, Pallas kernels for 0% -> 0%
where the time goes in v1:
time: 650 us; the launch traced here: 640 us
  waiting for transfers between devices  243 us (37%)
  blocking collectives  222 us (34%)
  matrix products  64.7 us (10%)
  local copies, waits for them, and re-layouts  40.6 us (6%)
  starting transfers between devices  34.9 us (5%)
  other arithmetic  19.9 us (3%)
  between operations  14.8 us (2%)
    reduce_scatter x2, waiting for transfers between devices, collect(): lax.psum_scatter(partial_sums[None], 'local', scatter_dimension=2, tiled=...  198 us
    all_to_all x2, blocking collectives, spread(): lax.all_to_all(jnp.stack([arrived] * lax.axis_size('local')), 'local', 0, 0)  152 us
    all_to_all x2, blocking collectives, spread(): lax.all_to_all(buffer, 'node', split_axis=0, concat_axis=2, tiled=True)  69.8 us
    all_to_all x4, waiting for transfers between devices, exchange_in_pieces(): lax.all_to_all(piece, axis, split_axis=0, concat_axis=0, tiled=True)  44.6 us
    all_to_all x4, starting transfers between devices, exchange_in_pieces(): lax.all_to_all(piece, axis, split_axis=0, concat_axis=0, tiled=True)  34.8 us
  transfers between devices with their start and end apart: 6, of which 6 were waited for; matrix products, arithmetic and copies ran while one was open for 4% of the time, Pallas kernels for 0%

profile of v1, /device:TPU:0, one launch (start us, length us, event | category | flops | bytes accessed | tf_op | source)
XLA Modules:
  0.0 639.6 jit_solution(6252686141998231283)
XLA Ops:
  13.5 3.5 reshape.166
  17.0 37.9 %all_to_all.48 = bf16[32,1,6,4096]{3,2,1,0:T(8,128)(2,1)} all-to-all(bf16[32,1,6,4096]{3,2,1,0:T(8,128)(2,1)} %bitcast.75), channel_id=1, replica_groups=mesh['node'=32,'local'=4] {'node'}, dimensions={0} | all-to-all | bytes 3145728 | tf_op jit(solution)/shard_map/all_to_all | solution.py:50
  54.9 3.7 stack.27
  60.8 77.1 %all_to_all.49 = bf16[4,1,1,192,4096]{4,3,2,1,0:T(8,128)(2,1)S(1)} all-to-all(bf16[4,1,1,192,4096]{4,3,2,1,0:T(8,128)(2,1)S(1)} %stack.28), channel_id=1, replica_groups=mesh['node'=32,'local'=4] {'local'}, dimensions={0} | all-to-all | bytes 12582912 | tf_op jit(solution)/shard_map/all_to_all | solution.py:52
  137.8 3.4 fusion.14
  142.0 4.5 multiply_convert_fusion.2
  147.3 6.3 convolution_bitcast_fusion
  153.7 101.3 %reduce-scatter.3.cloned.1.call-done = f32[1,1,192,4096]{3,2,1,0:T(8,128)} async-done(((f32[1,1,768,4096]{3,2,1,0:T(8,128)}), f32[1,1,192,4096]{3,2,1,0:T(8,128)}) %reduce-scatter.3.cloned.1.call-update) | async-done | bytes 3145744 | tf_op jit(solution)/shard_map/reduce_scatter | solution.py:58
  255.0 3.2 convert_element_type.66
  258.3 3.5 transpose_reshape.6
  261.8 4.7 slice_bitcast_fusion.3
  266.5 7.4 %all-to-all-start.2 = ((bf16[32,1,1,3,4096]{4,3,2,1,0:T(4,128)(2,1)}), bf16[32,1,1,3,4096]{4,3,2,1,0:T(4,128)(2,1)}, u32[]{:S(2)}, u32[]{:S(2)}) async-start(bf16[32,1,1,3,4096]{4,3,2,1,0:T(4,128)(2,1)} %get-tuple-element.18), calls=%async_computation.3 | async-start | bytes 2097152 | tf_op jit(solution)/shard_map/all_to_all | solution.py:33
  274.2 17.5 %all-to-all-done.2 = bf16[32,1,1,3,4096]{4,3,2,1,0:T(4,128)(2,1)} async-done(((bf16[32,1,1,3,4096]{4,3,2,1,0:T(4,128)(2,1)}), bf16[32,1,1,3,4096]{4,3,2,1,0:T(4,128)(2,1)}, u32[]{:S(2)}, u32[]{:S(2)}) %all-to-all-start.2) | async-done | bytes 786464 | tf_op jit(solution)/shard_map/all_to_all | solution.py:33
  291.7 15.2 %all-to-all-start.3 = ((bf16[32,1,1,3,4096]{4,3,2,1,0:T(4,128)(2,1)}), bf16[32,1,1,3,4096]{4,3,2,1,0:T(4,128)(2,1)}, u32[]{:S(2)}, u32[]{:S(2)}) async-start(bf16[32,1,1,3,4096]{4,3,2,1,0:T(4,128)(2,1)} %get-tuple-element.19), calls=%async_computation.4 | async-start | bytes 2097152 | tf_op jit(solution)/shard_map/all_to_all | solution.py:33
  307.2 16.5 %all-to-all-done.3 = bf16[32,1,1,3,4096]{4,3,2,1,0:T(4,128)(2,1)} async-done(((bf16[32,1,1,3,4096]{4,3,2,1,0:T(4,128)(2,1)}), bf16[32,1,1,3,4096]{4,3,2,1,0:T(4,128)(2,1)}, u32[]{:S(2)}, u32[]{:S(2)}) %all-to-all-start.3) | async-done | bytes 786464 | tf_op jit(solution)/shard_map/all_to_all | solution.py:33
  323.7 3.9 pad_maximum_fusion
  327.6 3.7 reshape_reshape.6
  338.4 3.5 reshape.171
  341.9 31.9 %all_to_all.50 = bf16[32,1,6,4096]{3,2,1,0:T(8,128)(2,1)} all-to-all(bf16[32,1,6,4096]{3,2,1,0:T(8,128)(2,1)} %bitcast.76), channel_id=1, replica_groups=mesh['node'=32,'local'=4] {'node'}, dimensions={0} | all-to-all | bytes 3145728 | tf_op jit(solution)/shard_map/all_to_all | solution.py:50
  373.8 3.7 stack.29
  379.7 75.2 %all_to_all.51 = bf16[4,1,1,192,4096]{4,3,2,1,0:T(8,128)(2,1)S(1)} all-to-all(bf16[4,1,1,192,4096]{4,3,2,1,0:T(8,128)(2,1)S(1)} %stack.30), channel_id=1, replica_groups=mesh['node'=32,'local'=4] {'local'}, dimensions={0} | all-to-all | bytes 12582912 | tf_op jit(solution)/shard_map/all_to_all | solution.py:52
  454.9 3.8 multiply_convert_fusion
  459.1 3.5 fusion.12
  462.6 6.4 %add_bitcast_fusion = f32[1,1,768,4096]{3,2,1,0:T(8,128)} fusion(f32[768,4096]{1,0:T(8,128)S(1)} %fusion.12, bf16[768,384]{1,0:T(8,128)(2,1)S(1)} %get-tuple-element.14, bf16[1,4096,384]{2,1,0:T(8,128)(2,1)S(1)} %copy-done.13), kind=kOutput, calls=%fused_computation | convolution fusion | flops 2419064832 | bytes 28901376 | tf_op jit(solution)/shard_map/erf,edf->erd/dot_general | solution.py:112
  473.6 96.8 %reduce-scatter.5.cloned.1.call-done = f32[1,1,192,4096]{3,2,1,0:T(8,128)} async-done(((f32[1,1,768,4096]{3,2,1,0:T(8,128)}), f32[1,1,192,4096]{3,2,1,0:T(8,128)}) %reduce-scatter.5.cloned.1.call-update) | async-done | bytes 3145744 | tf_op jit(solution)/shard_map/reduce_scatter | solution.py:58
  570.3 3.2 convert_element_type.74
  578.5 7.5 %all-to-all-start.6 = ((bf16[32,1,1,3,4096]{4,3,2,1,0:T(4,128)(2,1)}), bf16[32,1,1,3,4096]{4,3,2,1,0:T(4,128)(2,1)S(1)}, u32[]{:S(2)}, u32[]{:S(2)}) async-start(bf16[32,1,1,3,4096]{4,3,2,1,0:T(4,128)(2,1)} %get-tuple-element.16), calls=%async_computation.8 | async-start | bytes 2097152 | tf_op jit(solution)/shard_map/all_to_all | solution.py:33
  586.8 7.9 %fusion.1 = bf16[1,4096,384]{2,1,0:T(8,128)(2,1)} fusion(bf16[768,4096]{1,0:T(8,128)(2,1)} %bitcast.79, bf16[768,384]{1,0:T(8,128)(2,1)S(1)} %copy-done.18), kind=kOutput, calls=%fused_computation.8 | convolution fusion | flops 2417491968 | bytes 10027008 | tf_op jit(solution)/shard_map/erd,erf->edf/dot_general | solution.py:117
  594.7 8.9 %all-to-all-done.6 = bf16[32,1,1,3,4096]{4,3,2,1,0:T(4,128)(2,1)S(1)} async-done(((bf16[32,1,1,3,4096]{4,3,2,1,0:T(4,128)(2,1)}), bf16[32,1,1,3,4096]{4,3,2,1,0:T(4,128)(2,1)S(1)}, u32[]{:S(2)}, u32[]{:S(2)}) %all-to-all-start.6) | async-done | bytes 786464 | tf_op jit(solution)/shard_map/all_to_all | solution.py:33
  603.7 4.7 all-to-all-start.7
  608.4 7.2 %fusion.2 = bf16[1,384,4096]{2,1,0:T(8,128)(2,1)} fusion(bf16[768,384]{1,0:T(8,128)(2,1)S(1)} %copy-done.11, bf16[768,4096]{1,0:T(8,128)(2,1)} %bitcast.74), kind=kOutput, calls=%fused_computation.9 | convolution fusion | flops 2417491968 | bytes 10027008 | tf_op jit(solution)/shard_map/erf,erd->efd/dot_general | solution.py:120
  615.5 7.9 %fusion = bf16[1,4096,384]{2,1,0:T(8,128)(2,1)} fusion(bf16[768,4096]{1,0:T(8,128)(2,1)} %bitcast.80, bf16[768,384]{1,0:T(8,128)(2,1)S(1)} %copy-done.20), kind=kOutput, calls=%fused_computation.7 | convolution fusion | flops 2417491968 | bytes 10027008 | tf_op jit(solution)/shard_map/erd,erf->edf/dot_general | solution.py:114
  (98 shorter events, 39.5 us)
Async XLA Ops:
  7.2 140.2 %copy-start = (bf16[1,384,4096]{2,1,0:T(8,128)(2,1)S(1)}, bf16[1,384,4096]{2,1,0:T(8,128)(2,1)}, u32[]{:S(2)}) copy-start(bf16[1,384,4096]{2,1,0:T(8,128)(2,1)} %param.15) | copy-start | bytes 9437188
  7.2 247.8 %reduce-scatter.3.cloned.1.call-start = ((), (), s32[]{:S(2)}) async-start(), calls=%async_computation.10 | async-start | bytes 15728640 | tf_op jit(solution)/shard_map/reduce_scatter | solution.py:58
  9.9 1.9 copy-start.9
  60.8 77.1 %copy-start.14 = (bf16[1,4096,384]{2,1,0:T(8,128)(2,1)S(1)}, bf16[1,4096,384]{2,1,0:T(8,128)(2,1)}, u32[]{:S(2)}) copy-start(bf16[1,4096,384]{2,1,0:T(8,128)(2,1)} %param.13) | copy-start | bytes 9437188
  137.8 3.4 copy-start.8
  137.8 4.2 copy-start.12
  142.0 4.5 copy-start.22
  146.5 0.8 copy-start.10
  266.5 7.5 %copy-start.16 = (f32[128,128]{1,0:T(8,128)S(1)}, f32[128,128]{1,0:T(8,128)}, u32[]{:S(2)}) copy-start(f32[128,128]{1,0:T(8,128)} %param.10) | copy-start | bytes 196612
  266.5 25.3 %all-to-all-start.2 = ((bf16[32,1,1,3,4096]{4,3,2,1,0:T(4,128)(2,1)}), bf16[32,1,1,3,4096]{4,3,2,1,0:T(4,128)(2,1)}, u32[]{:S(2)}, u32[]{:S(2)}) async-start(bf16[32,1,1,3,4096]{4,3,2,1,0:T(4,128)(2,1)} %get-tuple-element.18), calls=%async_computation.3 | async-start | bytes 2097152 | tf_op jit(solution)/shard_map/all_to_all | solution.py:33
  291.7 32.0 %all-to-all-start.3 = ((bf16[32,1,1,3,4096]{4,3,2,1,0:T(4,128)(2,1)}), bf16[32,1,1,3,4096]{4,3,2,1,0:T(4,128)(2,1)}, u32[]{:S(2)}, u32[]{:S(2)}) async-start(bf16[32,1,1,3,4096]{4,3,2,1,0:T(4,128)(2,1)} %get-tuple-element.19), calls=%async_computation.4 | async-start | bytes 2097152 | tf_op jit(solution)/shard_map/all_to_all | solution.py:33
  306.9 263.4 %reduce-scatter.5.cloned.1.call-start = ((), (), s32[]{:S(2)}) async-start(), calls=%async_computation.11 | async-start | bytes 15728640 | tf_op jit(solution)/shard_map/reduce_scatter | solution.py:58
  331.3 2.1 copy-start.6
  331.3 2.2 copy-start.7
  333.5 2.2 copy-start.3
  333.5 2.2 copy-start.21
  379.7 75.2 %copy-start.23 = (f32[768,384]{1,0:T(8,128)S(1)}, f32[768,384]{1,0:T(8,128)}, u32[]{:S(2)}) copy-start(f32[768,384]{1,0:T(8,128)} %copy-done.22) | copy-start | bytes 3538948
  379.7 75.2 %copy-start.24 = (f32[768,384]{1,0:T(8,128)S(1)}, f32[768,384]{1,0:T(8,128)}, u32[]{:S(2)}) copy-start(f32[768,384]{1,0:T(8,128)} %get-tuple-element.27) | copy-start | bytes 3538948
  454.9 3.8 copy-start.2
  454.9 4.2 copy-start.15
  458.7 3.8 copy-start.19
  458.7 3.8 copy-start.17
  459.1 3.5 copy-start.13
  469.0 1.6 copy-start.4
  578.5 8.3 %copy-start.18 = (bf16[768,384]{1,0:T(8,128)(2,1)S(1)}, bf16[768,384]{1,0:T(8,128)(2,1)}, u32[]{:S(2)}) copy-start(bf16[768,384]{1,0:T(8,128)(2,1)} %copy-done.17) | copy-start | bytes 1769476
  578.5 25.2 %all-to-all-start.6 = ((bf16[32,1,1,3,4096]{4,3,2,1,0:T(4,128)(2,1)}), bf16[32,1,1,3,4096]{4,3,2,1,0:T(4,128)(2,1)S(1)}, u32[]{:S(2)}, u32[]{:S(2)}) async-start(bf16[32,1,1,3,4096]{4,3,2,1,0:T(4,128)(2,1)} %get-tuple-element.16), calls=%async_computation.8 | async-start | bytes 2097152 | tf_op jit(solution)/shard_map/all_to_all | solution.py:33
  594.7 13.6 %copy-start.11 = (bf16[768,384]{1,0:T(8,128)(2,1)S(1)}, bf16[768,384]{1,0:T(8,128)(2,1)}, u32[]{:S(2)}) copy-start(bf16[768,384]{1,0:T(8,128)(2,1)} %copy-done.10) | copy-start | bytes 1769476
  603.7 21.5 %all-to-all-start.7 = ((bf16[32,1,1,3,4096]{4,3,2,1,0:T(4,128)(2,1)}), bf16[32,1,1,3,4096]{4,3,2,1,0:T(4,128)(2,1)}, u32[]{:S(2)}, u32[]{:S(2)}) async-start(bf16[32,1,1,3,4096]{4,3,2,1,0:T(4,128)(2,1)} %get-tuple-element.17), calls=%async_computation.9 | async-start | bytes 2097152 | tf_op jit(solution)/shard_map/all_to_all | solution.py:33
  608.3 7.2 %copy-start.20 = (bf16[768,384]{1,0:T(8,128)(2,1)S(1)}, bf16[768,384]{1,0:T(8,128)(2,1)}, u32[]{:S(2)}) copy-start(bf16[768,384]{1,0:T(8,128)(2,1)} %copy-done.19) | copy-start | bytes 1769476
  628.9 2.1 copy-start.5
  628.9 3.5 copy-start.1
Sparse Core Ops, SparseCore 0:
  153.8 101.1 reduce-scatter.2
  469.1 101.1 reduce-scatter.4
